TPU v7x, 256 devices: a whole 4x4x8 slice. The times are simulated.
256 devices in a mesh: row: 16 (over x, y), col: 16 (over z, core).
Axes of the slice: x: 4, y: 4, z: 8, core: 2. Of those that a mesh axis runs over, the one named last changes fastest.
Arguments:
- panel_index: int32 [1], replicated, may hold values from 0 to 127
- coords: float32 [2, 8, 16, 128], P(None, None, 'row'), may hold values from 0 to 1
- region_ids: int32 [8, 16, 128], P(None, 'row'), may hold values from 0 to 15
- nugget: float32 [16], replicated, may hold values from 2 to 8
- variance: float32 [1], replicated, may hold values from 1 to 4
- length: float32 [1], replicated, may hold values from 0.02 to 0.06
- correction: float32 [8, 16, 128, 8, 16, 128], P(None, 'row', None, None, 'col'), may hold values from -0.5 to 0.5, as said below
- bin_index: int32 [8, 16, 16, 8], P(None, 'row', 'col'), may hold values from 0 to 4095
- fraction: float32 [8, 16, 16, 8], P(None, 'row', 'col'), may hold values from 0.05 to 0.95
- weights: float32 [8, 16, 16, 8], P(None, 'row', 'col'), may hold values from 0.5 to 6
Outputs:
- trailing: float32 [8, 16, 128, 8, 16, 128], P(None, 'row', None, None, 'col')
- panel: float32 [8, 16, 128, 128], P(None, 'row')
- scores_out: float32 [8, 16, 128], P(None, 'row')
- likelihood_terms: float32 [2], replicated
Inputs may be any that keep to these rules, and one draw needn't show every extreme that they name: correction is symmetric as a 16384 x 16384 matrix; in a diagonal tile (row tile equal to column tile) every entry has magnitude at most 0.015.
All inputs are finite; a program needn't handle non-finite values.
Results may differ from a plain program's by a relative error of at most 0.0003.
Values sent between devices are 32-bit elements; how exact they have to be, the bound alone decides.
A program may use at most 64 MiB of HBM per device.

v0:
```python
import jax
import jax.numpy as jnp
from jax import lax
from jax.sharding import PartitionSpec as P

NBINS = 4096
NREG = 16


ROOT_THREE = 1.7320508075688772
ROOT_TWO = 1.4142135623730951
HIGH = lax.Precision.HIGHEST


def from_root(block, axis, holder):
    block = jnp.where(lax.axis_index(axis) == holder, block, jnp.zeros_like(block))
    return lax.psum(block, axis)


def matern_kernel(first, second, variance, length):
    delta_x = first[0][:, None] - second[0][None, :]
    delta_y = first[1][:, None] - second[1][None, :]
    scaled = ROOT_THREE * jnp.sqrt(delta_x * delta_x + delta_y * delta_y) / length
    return variance * (1.0 + scaled) * jnp.exp(-scaled)


def pivot_factor(block, is_owner, pivot_scores):
    tile = block.shape[0]
    identity = jnp.eye(tile, dtype=jnp.float32)
    safe_block = jnp.where(is_owner, block, identity)
    factor = jnp.linalg.cholesky(safe_block)
    inverse = jax.scipy.linalg.solve_triangular(factor, identity, lower=True)
    log_diag = jnp.log(jnp.diagonal(factor))
    solved = jnp.dot(inverse, pivot_scores, precision=HIGH)
    return (inverse, log_diag, solved)


def column_panel(rows_panel, col_index, col_tiles, tile):
    every_row = lax.all_gather(rows_panel.reshape(-1, 1, tile, tile), "row", axis=1, tiled=True)
    return lax.dynamic_index_in_dim(every_row, col_index, 1, keepdims=False).reshape(
        col_tiles * tile, tile
    )


def on_device(
    panel_index,
    coords,
    region_ids,
    nugget,
    variance,
    length,
    correction,
    bin_index,
    fraction,
    weights,
):
    pivot = panel_index[0]
    n_row = lax.axis_size("row")
    n_col = lax.axis_size("col")
    row_index = lax.axis_index("row")
    col_index = lax.axis_index("col")
    row_tiles = coords.shape[1]
    tile = coords.shape[3]
    col_tiles = correction.shape[3]
    sub_sites = bin_index.shape[3]
    flat_bins = bin_index.reshape(-1)
    one_hot = (flat_bins[:, None] == jnp.arange(NBINS, dtype=jnp.int32)[None, :]).astype(
        jnp.float32
    )
    local_hist = jnp.dot(weights.reshape(-1), one_hot, precision=HIGH)
    hist = lax.psum(local_hist, ("row", "col"))
    total = jnp.sum(hist)
    before = jnp.cumsum(hist) - hist
    lookup = jnp.dot(one_hot, jnp.stack([before, hist], axis=1), precision=HIGH)
    prob = (lookup[:, 0] + fraction.reshape(-1) * lookup[:, 1]) / total
    local_scores = (ROOT_TWO * lax.erf_inv(2.0 * jnp.clip(prob, 0.01, 0.99) - 1.0)).reshape(
        row_tiles, 1, 1, sub_sites
    )
    row_scores = lax.all_gather(local_scores, "col", axis=2, tiled=True).reshape(row_tiles, tile)
    row_sites = coords.reshape(2, row_tiles * tile)
    every_site = lax.all_gather(coords, "row", axis=2, tiled=True)
    col_sites = lax.dynamic_index_in_dim(every_site, col_index, 2, keepdims=False).reshape(
        2, col_tiles * tile
    )
    row_ids = (
        (jnp.arange(row_tiles, dtype=jnp.int32)[:, None] * n_row + row_index) * tile
        + jnp.arange(tile, dtype=jnp.int32)[None, :]
    ).reshape(-1)
    col_ids = (
        (jnp.arange(col_tiles, dtype=jnp.int32)[:, None] * n_col + col_index) * tile
        + jnp.arange(tile, dtype=jnp.int32)[None, :]
    ).reshape(-1)
    regions = region_ids.reshape(-1)
    row_nugget = jnp.sum(
        jnp.where(
            regions[:, None] == jnp.arange(NREG, dtype=jnp.int32)[None, :], nugget[None, :], 0.0
        ),
        axis=1,
    )
    local_matrix = matern_kernel(row_sites, col_sites, variance[0], length[0])
    local_matrix = local_matrix + jnp.where(
        row_ids[:, None] == col_ids[None, :], row_nugget[:, None], 0.0
    )
    local_matrix = local_matrix - correction.reshape(row_tiles * tile, col_tiles * tile)
    pivot_row_dev = pivot % n_row
    pivot_col_dev = pivot % n_col
    pivot_row_tile = pivot // n_row
    pivot_col_tile = pivot // n_col
    own_column = lax.dynamic_slice_in_dim(local_matrix, pivot_col_tile * tile, tile, 1)
    pivot_scores = lax.dynamic_index_in_dim(row_scores, pivot_row_tile, 0, keepdims=False)
    is_owner = (row_index == pivot_row_dev) & (col_index == pivot_col_dev)
    block = lax.dynamic_slice_in_dim(own_column, pivot_row_tile * tile, tile, 0)
    inverse, log_diag, solved = pivot_factor(block, is_owner, pivot_scores)
    inverse, log_diag, solved = (
        from_root(inverse, "row", pivot_row_dev),
        from_root(log_diag, "row", pivot_row_dev),
        from_root(solved, "row", pivot_row_dev),
    )
    rows_panel = jnp.dot(own_column, inverse.T, precision=HIGH)
    rows_panel, log_diag, solved = (
        from_root(rows_panel, "col", pivot_col_dev),
        from_root(log_diag, "col", pivot_col_dev),
        from_root(solved, "col", pivot_col_dev),
    )
    cols_panel = column_panel(rows_panel, col_index, col_tiles, tile)
    trailing = local_matrix - jnp.dot(rows_panel, cols_panel.T, precision=HIGH)
    updated = row_scores - jnp.dot(rows_panel, solved, precision=HIGH).reshape(row_tiles, tile)
    replace = (jnp.arange(row_tiles, dtype=jnp.int32)[:, None] == pivot_row_tile) & (
        row_index == pivot_row_dev
    )
    updated = jnp.where(replace, solved[None, :], updated)
    likelihood_terms = jnp.stack([2.0 * jnp.sum(log_diag), jnp.dot(solved, solved, precision=HIGH)])
    return (
        trailing.reshape(row_tiles, 1, tile, col_tiles, 1, tile),
        rows_panel.reshape(row_tiles, 1, tile, tile),
        updated.reshape(row_tiles, 1, tile),
        likelihood_terms,
    )


def solution(mesh):
    in_specs = (
        P(),
        P(None, None, "row", None),
        P(None, "row", None),
        P(),
        P(),
        P(),
        P(None, "row", None, None, "col", None),
        P(None, "row", "col", None),
        P(None, "row", "col", None),
        P(None, "row", "col", None),
    )
    out_specs = (
        P(None, "row", None, None, "col", None),
        P(None, "row", None, None),
        P(None, "row", None),
        P(),
    )
    return jax.shard_map(
        on_device, mesh=mesh, in_specs=in_specs, out_specs=out_specs, check_vma=False
    )
```

profile of v0, /device:TPU:1, one launch (start us, length us, event | category | flops | bytes accessed | tf_op | source)
XLA Modules:
  0.0 456.2 jit_solution(7377401832000871921)
XLA Ops:
  8.0 0.7 fusion.22
  8.7 19.5 %all_gather.9 = f32[2,8,16,128]{3,1,0,2:T(8,128)S(1)} all-gather(f32[2,8,1,128]{3,1,0,2:T(8,128)} %bitcast.98), channel_id=1, replica_groups=mesh['row'=16,'col'=16] {'row'}, dimensions={2}, use_global_device_ids=true | all-gather | bytes 139264 | tf_op jit(solution)/shard_map/all_gather | solution.py:81
  29.6 0.8 select_reduce_fusion.1
  30.4 5.4 %bitcast_subtract_fusion = f32[1024,1024]{1,0:T(8,128)S(1)} fusion(f32[128,8,8,128]{3,2,1,0:T(8,128)} %bitcast.93, f32[1024]{0:T(1024)S(1)} %select_reduce_fusion.1, s32[1024]{0:T(1024)S(1)} %get-tuple-element.36, f32[]{:T(128)} %bitcast.90, f32[1024]{0:T(1024)S(1)} %get-tuple-element.29, f32[1024]{0:T(1024)S(1)} %bitcast.101, ...), kind=kLoop, calls=%fused_computation.1 | loop fusion | flops 15728640 | bytes 8417288 | tf_op jit(solution)/shard_map/sub | solution.py:104
  35.8 2.0 copy-done
  38.0 1.0 fusion.8
  39.0 11.7 %cholesky.18 = f32[128,128]{1,0:T(8,128)S(1)} custom-call(f32[128,128]{1,0:T(8,128)S(1)} %fusion.8), custom_call_target="Cholesky" | custom-call | tf_op jit(solution)/shard_map/jit(cholesky)/cholesky | solution.py:31
  50.7 0.6 compare_reduce_fusion
  51.4 0.7 select_bitcast_fusion
  52.1 9.8 %custom-call.7 = f32[1,128,128]{1,2,0:T(8,128)S(1)} custom-call(f32[1,128,128]{2,1,0:T(8,128)S(1)} %get-tuple-element.26), custom_call_target="InvertDiagBlocksLowerTriangular" | custom-call | tf_op jit(solution)/shard_map/jit(_solve_triangular)/triangular_solve | solution.py:32
  61.9 0.9 broadcast_select_fusion
  62.8 95.8 %all-reduce.5.cloned.1.call-done = f32[128,128]{1,0:T(8,128)} async-done(((f32[128,128]{1,0:T(8,128)}), f32[128,128]{1,0:T(8,128)}) %all-reduce.5.cloned.1.call-update) | async-done | bytes 65552 | tf_op jit(solution)/shard_map/psum | solution.py:17
  158.6 2.4 convolution_select_fusion
  161.1 111.1 %all-reduce.7.cloned.1.call-done = f32[1024,128]{1,0:T(8,128)} async-done(((f32[1024,128]{1,0:T(8,128)}), f32[1024,128]{1,0:T(8,128)}) %all-reduce.7.cloned.1.call-update) | async-done | bytes 524304 | tf_op jit(solution)/shard_map/psum | solution.py:17
  272.8 0.7 reduce.27
  274.0 0.7 reduce.28
  275.3 78.9 %psum.51 = f32[4096]{0:T(1024)S(1)} all-reduce(f32[4096]{0:T(1024)S(1)} %bitcast.103), channel_id=1, replica_groups=mesh['row'=16,'col'=16] {'row','col'}, use_global_device_ids=true, to_apply=%region_5.6 | all-reduce | flops 4096 | bytes 32768 | tf_op jit(solution)/shard_map/psum | solution.py:71
  354.7 0.6 fusion.21
  355.3 0.7 fusion.1
  356.1 0.7 multiply_bitcast_fusion
  356.8 15.4 %all_gather.11 = f32[8,1,16,8]{3,0,1,2:T(8,128)S(1)} all-gather(f32[8,1,1,8]{3,0,1,2:T(8,128)S(1)} %multiply_bitcast_fusion), channel_id=1, replica_groups=mesh['row'=16,'col'=16] {'col'}, dimensions={2}, use_global_device_ids=true | all-gather | bytes 4352 | tf_op jit(solution)/shard_map/all_gather | solution.py:79
  372.5 1.2 gather_fusion
  373.9 29.7 %all-reduce.1 = (f32[128]{0:T(128)S(1)}, f32[128]{0:T(128)S(1)}) all-reduce(f32[128]{0:T(128)S(1)} %fusion, f32[128]{0:T(128)S(1)} %broadcast_select_fusion.1), channel_id=1, replica_groups=mesh['row'=16,'col'=16] {'row'}, use_global_device_ids=true, to_apply=%region_9.10 | all-reduce | flops 256 | bytes 2048 | tf_op jit(solution)/shard_map/psum | solution.py:17
  403.6 30.3 %all-reduce = (f32[128]{0:T(128)S(1)}, f32[128]{0:T(128)S(1)}) all-reduce(f32[128]{0:T(128)S(1)} %broadcast_select_fusion.3, f32[128]{0:T(128)S(1)} %broadcast_select_fusion.2), channel_id=1, replica_groups=mesh['row'=16,'col'=16] {'col'}, use_global_device_ids=true, to_apply=%region_10.11 | all-reduce | flops 256 | bytes 2048 | tf_op jit(solution)/shard_map/psum | solution.py:17
  433.9 0.6 reduce_sum.29
  435.8 1.2 pad_maximum_fusion
  437.0 1.6 fusion.18
  438.6 0.7 subtract_select_fusion
  439.3 1.1 constant_dynamic-slice_fusion.1
  440.4 5.5 %subtract_bitcast_fusion = f32[128,8,8,128]{3,1,2,0:T(8,128)S(1)} fusion(f32[1024,1024]{1,0:T(8,128)} %copy-done, f32[1024,128]{1,0:T(8,128)S(1)} %copy-done.1, f32[1024,128]{1,0:T(8,128)S(1)} %bitcast.95), kind=kOutput, calls=%fused_computation.2 | convolution fusion | flops 1611661312 | bytes 9437184 | tf_op jit(solution)/shard_map/dot_general | solution.py:126
  445.9 3.0 copy.46
  448.9 0.8 copy.53
  (45 shorter events, 3.9 us)
Async XLA Ops:
  7.2 151.4 %all-reduce.5.cloned.1.call-start = ((), (), s32[]{:S(2)}) async-start(), calls=%async_computation | async-start | bytes 131072 | tf_op jit(solution)/shard_map/psum | solution.py:17
  30.4 242.4 %copy-start.2 = (s32[8,1,1,8]{3,2,1,0:T(1,128)S(1)}, s32[8,1,1,8]{3,2,1,0:T(1,128)}, u32[]{:S(2)}) copy-start(s32[8,1,1,8]{3,2,1,0:T(1,128)} %param.17) | copy-start | bytes 772
  30.4 243.6 %copy-start.3 = (f32[8,1,1,8]{3,2,1,0:T(1,128)S(1)}, f32[8,1,1,8]{3,2,1,0:T(1,128)}, u32[]{:S(2)}) copy-start(f32[8,1,1,8]{3,2,1,0:T(1,128)} %param.19) | copy-start | bytes 772
  30.4 325.7 %copy-start.4 = (f32[8,1,1,8]{3,2,1,0:T(1,128)S(1)}, f32[8,1,1,8]{3,2,1,0:T(1,128)}, u32[]{:S(2)}) copy-start(f32[8,1,1,8]{3,2,1,0:T(1,128)} %param.18) | copy-start | bytes 772
  35.8 2.0 copy-start
  62.8 209.4 %all-reduce.7.cloned.1.call-start = ((), (), s32[]{:S(2)}) async-start(), calls=%async_computation.1 | async-start | bytes 1048576 | tf_op jit(solution)/shard_map/psum | solution.py:17
  161.0 278.3 %all-gather.2.cloned.1.call-start = ((), (), s32[]{:S(2)}) async-start(), calls=%async_computation.2 | async-start | bytes 8912896 | tf_op jit(solution)/shard_map/all_gather | solution.py:39
  272.2 168.2 %copy-start.1 = (f32[1024,128]{1,0:T(8,128)S(1)}, f32[1024,128]{1,0:T(8,128)}, u32[]{:S(2)}) copy-start(f32[1024,128]{1,0:T(8,128)} %all-reduce.7.cloned.1.call-done) | copy-start | bytes 1572868
Sparse Core Ops, SparseCore 0:
  62.9 95.6 all-reduce.4
  161.6 110.5 all-reduce.6
  274.7 76.6 all-gather.1
where the time goes:
time: 457 us; the launch traced here: 456 us
  waiting for transfers between devices  207 us (45%)
  blocking collectives  174 us (38%)
  other arithmetic  36.3 us (8%)
  between operations  16.6 us (4%)
  matrix products  11.7 us (3%)
  local copies, waits for them, and re-layouts  10.7 us (2%)
    psum x2, waiting for transfers between devices, from_root(): return lax.psum(block, axis)  207 us
    psum x1, blocking collectives, on_device(): hist = lax.psum(local_hist, ('row', 'col'))  78.9 us
    psum x2, blocking collectives, from_root(): return lax.psum(block, axis)  60 us
    all_gather x1, blocking collectives, on_device(): every_site = lax.all_gather(coords, 'row', axis=2, tiled=True)  19.5 us
    all_gather x1, blocking collectives, on_device(): lax.all_gather(local_scores, 'col', axis=2, tiled=True)  15.4 us
    another operation x3, other arithmetic, pivot_factor(): factor = jnp.linalg.cholesky(safe_block)  12.4 us
    another operation x2, other arithmetic, pivot_factor(): inverse = jax.scipy.linalg.solve_triangular(factor, identity, lower=True)  10.5 us
  transfers between devices with their start and end apart: 3, of which 2 were waited for; matrix products, arithmetic and copies ran while one was open for 3% of the time, Pallas kernels for 0%

commit v1 on v0

v1 whole, which is shorter than its diff:
```python
import functools

import jax
import jax.numpy as jnp
from jax import lax
from jax.experimental import pallas as pl
from jax.experimental.pallas import tpu as pltpu
from jax.sharding import PartitionSpec as P

F32 = jnp.float32
BF16 = jnp.bfloat16
I32 = jnp.int32
MESH = pl.DeviceIdType.MESH
N = 16
NREG = 16
ROOT_THREE = 1.7320508075688772
ROOT_TWO = 1.4142135623730951
NT = (((1,), (1,)), ((), ()))
NN = (((1,), (0,)), ((), ()))
TN = (((0,), (0,)), ((), ()))
PIECE = 64
MIB = 2**20


def iota(shape, dim):
    return lax.broadcasted_iota(I32, shape, dim)


def split2(x):
    high = x.astype(BF16)
    return high, (x - high.astype(F32)).astype(BF16)


def split3(x):
    high = x.astype(BF16)
    rest = x - high.astype(F32)
    mid = rest.astype(BF16)
    return high, mid, (rest - mid.astype(F32)).astype(BF16)


def dot3(a, b, dims):
    (ca,), (cb,) = dims[0]
    ah, al = split2(a)
    bh, bl = split2(b)
    return lax.dot_general(
        jnp.concatenate([ah, ah, al], axis=ca),
        jnp.concatenate([bh, bl, bh], axis=cb),
        dims,
        preferred_element_type=F32,
    )


def matern(dx, dy, variance):
    scaled = jnp.sqrt(dx * dx + dy * dy)
    return (variance + variance * scaled) * jnp.exp(-scaled)


def factor_inverse(work, inv):
    nb = 16
    groups = nb // 8
    sub = iota((8, 128), 0)
    lane = iota((nb, 128), 1)
    inv[...] = (iota((128, 128), 0) == iota((128, 128), 1)).astype(F32)

    def block(p, carry):
        rows_k = [work[8 * g : 8 * g + 8, :] for g in range(groups)]
        rows_i = [inv[8 * g : 8 * g + 8, :] for g in range(groups)]
        col = [
            [
                jnp.broadcast_to(rows_k[g][:, q : q + 1], (8, 128)) if 8 * g + 7 >= q else None
                for g in range(groups)
            ]
            for q in range(nb)
        ]
        pivots = [jnp.ones((8, 128), F32) for _ in range(groups)]
        for j in range(nb):
            gj, sj = divmod(j, 8)
            pivot = jnp.broadcast_to(col[j][gj][sj : sj + 1, :], (8, 128))
            pivots[gj] = jnp.where(sub == sj, pivot, pivots[gj])
            if j == nb - 1:
                break
            recip = 1.0 / pivot
            mult = [None] * groups
            for g in range(gj, groups):
                m = col[j][g] * recip
                mult[g] = jnp.where(sub > sj, m, 0.0) if g == gj else m
            for q in range(j + 1, nb):
                gq, sq = divmod(q, 8)
                scale = jnp.broadcast_to(col[j][gq][sq : sq + 1, :], (8, 128))
                for g in range(gq, groups):
                    col[q][g] = col[q][g] - mult[g] * scale
            row_k = jnp.broadcast_to(rows_k[gj][sj : sj + 1, :], (8, 128))
            row_i = jnp.broadcast_to(rows_i[gj][sj : sj + 1, :], (8, 128))
            for g in range(gj, groups):
                if 8 * g + 7 > j:
                    rows_k[g] = rows_k[g] - mult[g] * row_k
                    rows_i[g] = rows_i[g] - mult[g] * row_i
        roots = [lax.rsqrt(x) for x in pivots]
        upper = jnp.concatenate([rows_k[g] * roots[g] for g in range(groups)], axis=0)
        done = jnp.concatenate([rows_i[g] * roots[g] for g in range(groups)], axis=0)
        below = jnp.where((lane >= nb) & (lane < 128 - nb * p), upper, 0.0)
        h, m, l = split3(below)
        h2, m2, l2 = split3(done)
        left = jnp.concatenate([h, h, m, m, h, l], axis=0)
        right = jnp.concatenate(
            [
                jnp.concatenate([h, m, h, m, l, h], axis=0),
                jnp.concatenate([h2, m2, h2, m2, l2, h2], axis=0),
            ],
            axis=1,
        )
        update = lax.dot_general(left, right, TN, preferred_element_type=F32)
        next_k = work[nb:, :] - update[nb:, :128]
        next_i = inv[nb:, :] - update[nb:, 128:]
        work[0 : 128 - nb, :] = pltpu.roll(next_k, 128 - nb, 1)
        inv[0 : 128 - nb, :] = next_i
        inv[128 - nb :, :] = done
        return carry

    lax.fori_loop(0, 128 // nb, block, 0)


def exchange_kernel(
    d,
    k_ref,
    nugget_ref,
    variance_ref,
    length_ref,
    coords_s,
    coords_ref,
    regions_ref,
    bins_ref,
    fraction_ref,
    weights_ref,
    corr_hbm,
    matrix_hbm,
    rows_out,
    cols_out,
    inverse_out,
    hist_out,
    sites_out,
    pivot_out,
    corr,
    row_raw,
    col_raw,
    work,
    inverse,
    factor_rx,
    col_sites,
    pivot_info,
    obs,
    hist,
    hist_rx,
    hist_all,
    sites,
    pivot_obs,
    in_sem,
    out_sem,
    send,
    recv,
    row_recv,
):
    r = lax.axis_index("row")
    c = lax.axis_index("col")
    sibling = c + 1 - 2 * lax.rem(c, 2)
    tile_at = jnp.full((128, 128), k_ref[0] // N, I32)
    (
        S_SITES, S_PIVOT, S_OBS, S_F1, S_F2, S_F3, S_H2, S_H3, S_PO, S_R1, S_R2, S_R3, S_C1, S_C2,
    ) = range(14)

    def row_peer(i):
        return lax.rem(r + i, N)

    def col_peer(i):
        return lax.rem(c + i, N)

    def send_to(src, dst, which, to, sem=None):
        pltpu.make_async_remote_copy(
            src_ref=src,
            dst_ref=dst,
            send_sem=send.at[which],
            recv_sem=recv.at[which] if sem is None else sem,
            device_id=to,
            device_id_type=MESH,
        ).start()

    def wait(ref, sem):
        pltpu.make_async_copy(ref, ref, sem).wait()

    def each_peer(body):
        def step(i, carry):
            body(i)
            return carry

        lax.fori_loop(1, N, step, 0)

    def rows8(ref, i):
        return ref.at[pl.ds(pl.multiple_of(i * 8, 8), 8)]

    def piece(ref, i):
        return ref.at[pl.ds(pl.multiple_of(i * PIECE, PIECE), PIECE)]

    barrier = pltpu.get_barrier_semaphore()

    def greet(i):
        pl.semaphore_signal(barrier, inc=1, device_id=(row_peer(i), c), device_id_type=MESH)
        pl.semaphore_signal(barrier, inc=1, device_id=(r, col_peer(i)), device_id_type=MESH)

    each_peer(greet)
    load = pltpu.make_async_copy(corr_hbm, corr, in_sem)
    load.start()

    factor = ROOT_THREE / length_ref[0]
    variance = variance_ref[0]
    regions = regions_ref[...]
    nugget = jnp.zeros((8, 128), F32)
    for g in range(NREG):
        nugget = jnp.where(regions == g, nugget_ref[g], nugget)
    obs[0] = jnp.concatenate(
        [bins_ref[...].astype(F32), fraction_ref[...], weights_ref[...], jnp.zeros((8, 104), F32)],
        axis=1,
    )
    pad = jnp.zeros((120, 128), F32)
    x_rows = jnp.transpose(jnp.concatenate([coords_ref[0], pad], axis=0)) * factor
    y_rows = jnp.transpose(jnp.concatenate([coords_ref[1], pad], axis=0)) * factor
    diagonal = iota((128, 128), 0) == iota((128, 128), 1)

    def pick_row(x):
        return jnp.sum(jnp.where(iota((8, 128), 0) == tile_at[0:8], x, 0.0), axis=0, keepdims=True)

    def pick(tiles, rows):
        found = tiles(0)
        for b in range(1, 8):
            found = jnp.where(tile_at[0:rows] == b, tiles(b), found)
        return found

    @pl.when(r == d)
    def _():
        pivot_info[...] = jnp.concatenate(
            [
                pick_row(coords_ref[0]),
                pick_row(coords_ref[1]),
                pick_row(nugget),
                jnp.zeros((5, 128), F32),
            ],
            axis=0,
        )

    load.wait()

    @pl.when(c == d)
    def _():
        def rows_of(i, carry):
            row_raw[pl.ds(pl.multiple_of(i * 32, 32), 32), :] = pick(
                lambda b: corr[pl.ds(i * 256 + b, 32, stride=8), :], 32
            )
            return carry

        lax.fori_loop(0, 32, rows_of, 0)

    @pl.when(r == d)
    def _():
        def cols_of(i, carry):
            at = pl.multiple_of(i * 32, 32)
            col_raw[pl.ds(at, 32), :] = pick(lambda b: corr[pl.ds(b * 1024 + at, 32), :], 32)
            return carry

        lax.fori_loop(0, 32, cols_of, 0)

    @pl.when((r == d) & (c == d))
    def _():
        info = pivot_info[...]
        across = jnp.transpose(info)
        px = info[0:1, :] * factor
        py = info[1:2, :] * factor
        tile = matern(across[:, 0:1] * factor - px, across[:, 1:2] * factor - py, variance)
        work[...] = tile + jnp.where(diagonal, info[2:3, :], 0.0)

        def own_tile(i, carry):
            at = pl.ds(pl.multiple_of(i * 32, 32), 32)
            work[at, :] = work[at, :] - pick(lambda b: row_raw[pl.ds(b * 128 + i * 32, 32), :], 32)
            return carry

        lax.fori_loop(0, 4, own_tile, 0)
        factor_inverse(work, inverse)
        factor_rx[8 * d : 8 * d + 8, :] = inverse[8 * d : 8 * d + 8, :]

    pl.semaphore_wait(barrier, 2 * (N - 1))

    @pl.when(r == d)
    def _():
        each_peer(lambda i: send_to(pivot_info, pivot_info, S_PIVOT, (row_peer(i), c)))

    @pl.when(r == c)
    def _():
        each_peer(lambda i: send_to(coords_ref, col_sites, S_SITES, (row_peer(i), c)))
        col_sites[...] = coords_ref[...]

    @pl.when((r == d) & (c == d))
    def _():
        each_peer(
            lambda i: send_to(
                rows8(inverse, col_peer(i)), rows8(factor_rx, col_peer(i)), S_F1, (r, col_peer(i))
            )
        )

    each_peer(lambda i: send_to(obs.at[0], obs.at[i], S_OBS, (r, col_peer(i))))

    @pl.when(r == d)
    def _():
        each_peer(
            lambda i: send_to(
                piece(col_raw, row_peer(i)), piece(col_raw, row_peer(i)), S_C1, (row_peer(i), c)
            )
        )

    @pl.when(c == d)
    def _():
        each_peer(
            lambda i: send_to(
                piece(row_raw, col_peer(i)), piece(row_raw, col_peer(i)), S_R1, (r, col_peer(i))
            )
        )

    @pl.when((r == d) & (c != d))
    def _():
        wait(rows8(factor_rx, c), recv.at[S_F1])

    @pl.when(r == d)
    def _():
        each_peer(
            lambda i: send_to(rows8(factor_rx, c), rows8(factor_rx, c), S_F2, (row_peer(i), c))
        )

    def share_row(i):
        to = col_peer(2 * i)

        @pl.when(to != d)
        def _():
            send_to(piece(row_raw, c), piece(row_raw, c), S_R2, (r, to), row_recv.at[c // 2])

    @pl.when(c != d)
    def _():
        wait(piece(row_raw, c), recv.at[S_R1])

    def share_row_step(i, carry):
        share_row(i)
        return carry

    lax.fori_loop(1, 8, share_row_step, 0)

    @pl.when(sibling != d)
    def _():
        send_to(piece(row_raw, c), piece(row_raw, c), S_R3, (r, sibling))

    @pl.when(r != d)
    def _():
        wait(piece(col_raw, r), recv.at[S_C1])

    def share_col(i):
        @pl.when(row_peer(i) != d)
        def _():
            send_to(piece(col_raw, r), piece(col_raw, r), S_C2, (row_peer(i), c))

    each_peer(share_col)

    wait(obs.at[pl.ds(1, 15)], recv.at[S_OBS])
    lane = iota((8, 128), 1)

    def unpack(i, found):
        source = lax.rem(c - i + N, N)
        packed = obs[i]
        here = (lane // 8) == source
        return tuple(
            jnp.where(here, pltpu.roll(packed, lax.rem(8 * source - 8 * j + 128, 128), 1), found[j])
            for j in range(3)
        )

    found = lax.fori_loop(0, N, unpack, tuple(jnp.zeros((8, 128), F32) for _ in range(3)))
    for j in range(3):
        sites[j] = found[j]

    @pl.when(r == d)
    def _():
        pivot_obs[...] = jnp.concatenate(
            [
                pick_row(found[0]),
                pick_row(found[1]),
                jnp.zeros((6, 128), F32),
            ],
            axis=0,
        )
        each_peer(lambda i: send_to(pivot_obs, pivot_obs, S_PO, (row_peer(i), c)))

    level = iota((128, 128), 0)

    def count(a, total):
        bins_i = sites[0, pl.ds(a, 1), :].astype(I32)
        high_i = (bins_i // 256) * 8 + (bins_i // 128) % 2
        weighted = jnp.where(level == high_i, sites[2, pl.ds(a, 1), :], 0.0)
        wh, wl = split2(weighted)
        low = (level == bins_i % 128).astype(F32).astype(BF16)
        return total + lax.dot_general(
            jnp.concatenate([wh, wl], axis=1),
            jnp.concatenate([low, low], axis=1),
            NT,
            preferred_element_type=F32,
        )

    hist[...] = lax.fori_loop(0, 8, count, jnp.zeros((128, 128), F32))
    each_peer(lambda i: send_to(rows8(hist, c), hist_rx.at[i], S_H2, (row_peer(i), c)))

    @pl.when(r != d)
    def _():
        wait(rows8(factor_rx, c), recv.at[S_F2])

    each_peer(lambda i: send_to(rows8(factor_rx, c), rows8(factor_rx, c), S_F3, (r, col_peer(i))))

    def pass_on(i):
        source = lax.rem(c + 16 - 2 * i, N)
        wait(piece(row_raw, source), row_recv.at[source // 2])

        @pl.when(sibling != d)
        def _():
            send_to(piece(row_raw, source), piece(row_raw, source), S_R3, (r, sibling))

    def pass_own(i):
        source = lax.rem(c + 16 - 2 * i, N)
        send_to(piece(row_raw, source), piece(row_raw, source), S_R3, (r, sibling))

    def pass_piece(i):
        @pl.when(c != d)
        def _():
            pass_on(i)

        @pl.when(c == d)
        def _():
            pass_own(i)

    @pl.when(r != c)
    def _():
        wait(col_sites, recv.at[S_SITES])

    col_x = col_sites[0] * factor
    col_y = col_sites[1] * factor
    place = iota((8, 128), 0) * 128 + lane
    own_nugget = jnp.where(r == c, nugget, 0.0)

    def form(a, carry_a):
        def eight(q, carry):
            for u in range(8):
                t = q * 8 + u
                at = pl.ds(pl.multiple_of(a * 1024 + t * 8, 8), 8)
                value = matern(
                    coords_s[0, a, t] * factor - col_x, coords_s[1, a, t] * factor - col_y, variance
                )
                value = value + jnp.where(place == a * 128 + t, own_nugget, 0.0)
                corr[at, :] = value - corr[at, :]
            return carry

        lax.fori_loop(0, 16, eight, 0)
        at = pl.ds(pl.multiple_of(a * 1024, 1024), 1024)
        pltpu.make_async_copy(corr.at[at], matrix_hbm.at[at], out_sem).start()


        @pl.when(a == 2)
        def _():
            wait(hist_rx.at[pl.ds(1, 15)], recv.at[S_H2])
            own = pl.ds(pl.multiple_of(c * 8, 8), 8)
            hist_all[own, :] = lax.fori_loop(
                1, N, lambda i, total: total + hist_rx[i], hist[own, :]
            )
            each_peer(
                lambda i: send_to(rows8(hist_all, c), rows8(hist_all, c), S_H3, (r, col_peer(i)))
            )

        @pl.when(a >= 1)
        def _():
            pass_piece(a)

        return carry_a

    lax.fori_loop(0, 8, form, 0)

    @pl.when(r != d)
    def _():
        wait(pivot_info, recv.at[S_PIVOT])

    info = pivot_info[...]
    across = jnp.transpose(info)
    px = info[0:1, :] * factor
    py = info[1:2, :] * factor
    pnug = jnp.where(diagonal, info[2:3, :], 0.0)
    tx = across[:, 0:1] * factor
    ty = across[:, 1:2] * factor

    def panels(a, carry):
        at = pl.ds(pl.multiple_of(a * 128, 128), 128)
        turn = lax.rem(128 - a, 128)
        x = pltpu.roll(x_rows, turn, 1)[:, 0:1]
        y = pltpu.roll(y_rows, turn, 1)[:, 0:1]
        extra = jnp.where(tile_at == a, pnug, 0.0)
        rows_out[at, :] = matern(x - px, y - py, variance) + jnp.where(r == d, extra, 0.0)
        x = col_sites[0, pl.ds(a, 1), :] * factor
        y = col_sites[1, pl.ds(a, 1), :] * factor
        cols_out[a] = matern(tx - x, ty - y, variance) + jnp.where(c == d, extra, 0.0)
        return carry

    lax.fori_loop(0, 8, panels, 0)

    @pl.when(r != d)
    def _():
        wait(col_raw.at[pl.ds(0, 15 * PIECE)], recv.at[S_C2])
        wait(pivot_obs, recv.at[S_PO])


    def less_cols(b, carry):
        cols_out[b] = cols_out[b] - col_raw[pl.ds(b, 128, stride=8), :]
        return carry

    lax.fori_loop(0, 8, less_cols, 0)
    sites_out[...] = sites[...]
    pivot_out[...] = pivot_obs[...]
    wait(factor_rx.at[pl.ds(0, 120)], recv.at[S_F3])
    inverse_out[...] = factor_rx[...]
    wait(hist_all.at[pl.ds(0, 120)], recv.at[S_H3])
    hist_out[...] = hist_all[...]

    @pl.when(c != d)
    def _():
        wait(row_raw.at[pl.ds(0, 8 * PIECE)], recv.at[S_R3])

    def less_rows(a, carry):
        at = pl.ds(pl.multiple_of(a * 128, 128), 128)
        rows_out[at, :] = rows_out[at, :] - row_raw[at, :]
        return carry

    lax.fori_loop(0, 8, less_rows, 0)

    def sent(ref, which):
        wait(ref, send.at[which])

    @pl.when(r == d)
    def _():
        sent(hist.at[pl.ds(0, 120)], S_PIVOT)
        sent(hist.at[pl.ds(0, 120)], S_F2)
        sent(hist.at[pl.ds(0, 120)], S_PO)
        sent(col_raw.at[pl.ds(0, 15 * PIECE)], S_C1)
        sent(col_raw.at[pl.ds(0, 15 * PIECE)], S_C2)

    @pl.when(r != d)
    def _():
        sent(col_raw.at[pl.ds(0, 14 * PIECE)], S_C2)

    @pl.when(r == c)
    def _():
        sent(row_raw.at[pl.ds(0, 240)], S_SITES)

    @pl.when((r == d) & (c == d))
    def _():
        sent(hist.at[pl.ds(0, 120)], S_F1)

    @pl.when(c == d)
    def _():
        sent(row_raw.at[pl.ds(0, 15 * PIECE)], S_R1)

    for which in (S_OBS, S_F3, S_H2, S_H3):
        sent(hist.at[pl.ds(0, 120)], which)

    same_place = lax.rem(c, 2) == d % 2

    @pl.when(same_place & (c != d))
    def _():
        sent(row_raw.at[pl.ds(0, 6 * PIECE)], S_R2)

    @pl.when(jnp.logical_not(same_place) | (c == d))
    def _():
        sent(row_raw.at[pl.ds(0, 7 * PIECE)], S_R2)

    @pl.when(sibling != d)
    def _():
        sent(row_raw.at[pl.ds(0, 8 * PIECE)], S_R3)

    wait(corr, out_sem)


def exchange(d, *args):
    vmem = pl.BlockSpec(memory_space=pltpu.VMEM)
    smem = pl.BlockSpec(memory_space=pltpu.SMEM)
    hbm = pl.BlockSpec(memory_space=pl.ANY)
    shape = lambda *s: jax.ShapeDtypeStruct(s, F32)
    return pl.pallas_call(
        functools.partial(exchange_kernel, d),
        out_shape=(
            shape(8192, 128),
            shape(1024, 128),
            shape(8, 128, 128),
            shape(128, 128),
            shape(128, 128),
            shape(3, 8, 128),
            shape(8, 128),
        ),
        in_specs=[smem] * 5 + [vmem] * 5 + [hbm],
        out_specs=(hbm,) + (vmem,) * 6,
        scratch_shapes=[
            pltpu.VMEM((8192, 128), F32),
            pltpu.VMEM((1024, 128), F32),
            pltpu.VMEM((1024, 128), F32),
            pltpu.VMEM((128, 128), F32),
            pltpu.VMEM((128, 128), F32),
            pltpu.VMEM((128, 128), F32),
            pltpu.VMEM((2, 8, 128), F32),
            pltpu.VMEM((8, 128), F32),
            pltpu.VMEM((N, 8, 128), F32),
            pltpu.VMEM((128, 128), F32),
            pltpu.VMEM((N, 8, 128), F32),
            pltpu.VMEM((128, 128), F32),
            pltpu.VMEM((3, 8, 128), F32),
            pltpu.VMEM((8, 128), F32),
            pltpu.SemaphoreType.DMA,
            pltpu.SemaphoreType.DMA,
            pltpu.SemaphoreType.DMA((14,)),
            pltpu.SemaphoreType.DMA((14,)),
            pltpu.SemaphoreType.DMA((8,)),
        ],
        compiler_params=pltpu.CompilerParams(
            collective_id=d, has_side_effects=True, vmem_limit_bytes=24 * MIB
        ),
        name="exchange",
    )(*args)


def quantile(x):
    w = -jnp.log((1.0 - x) * (1.0 + x)) - 2.5
    p = jnp.full_like(w, 2.81022636e-08)
    for coefficient in (
        3.43273939e-07,
        -3.5233877e-06,
        -4.39150654e-06,
        0.00021858087,
        -0.00125372503,
        -0.00417768164,
        0.246640727,
        1.50140941,
    ):
        p = coefficient + p * w
    return p * x


def update_kernel(
    k_ref,
    matrix_ref,
    rows_ref,
    cols_ref,
    inverse_ref,
    hist_ref,
    sites_ref,
    pivot_ref,
    trailing_ref,
    panel_ref,
    scores_ref,
    terms_ref,
    cols_panel,
    scores,
    solved,
):
    a = pl.program_id(0)
    inverse = inverse_ref[...]

    @pl.when(a == 0)
    def _():
        cols = jnp.concatenate([cols_ref[b] for b in range(8)], axis=1)
        panel = dot3(inverse, cols, NN)
        high, low = split2(panel)
        cols_panel[0:128, :] = high
        cols_panel[128:256, :] = low
        cols_panel[256:384, :] = high

        counts = hist_ref[...]
        level = iota((128, 128), 0)
        across = iota((128, 128), 1)
        parts = split3(counts)
        ahead = (across < level).astype(F32).astype(BF16)
        earlier = (level < across).astype(F32).astype(BF16)
        above = jnp.zeros((128, 128), F32)
        along = jnp.zeros((128, 128), F32)
        for part in parts:
            above = above + lax.dot_general(ahead, part, NN, preferred_element_type=F32)
            along = along + lax.dot_general(part, earlier, NN, preferred_element_type=F32)
        before = jnp.sum(above, axis=1, keepdims=True) + along
        total = jnp.sum(jnp.sum(counts, axis=1, keepdims=True), axis=0, keepdims=True)

        bins_f = jnp.concatenate([sites_ref[0], pivot_ref[...]], axis=0)
        fraction = jnp.concatenate([sites_ref[1], pivot_ref[...]], axis=0)
        bins_i = bins_f.astype(I32)
        high_i = (bins_i // 256) * 8 + (bins_i // 128) % 2
        low_i = bins_i % 128
        high_hot = jnp.concatenate(
            [(level == high_i[i : i + 1, :]).astype(F32).astype(BF16) for i in range(9)], axis=1
        )
        tripled = jnp.concatenate([high_hot] * 3, axis=0)
        look = [
            lax.dot_general(
                jnp.concatenate(split3(table), axis=0), tripled, TN, preferred_element_type=F32
            )
            for table in (before, counts)
        ]
        probs = []
        for i in range(9):
            hot = level == low_i[i : i + 1, :]
            at = slice(i * 128, (i + 1) * 128)
            start = jnp.sum(jnp.where(hot, look[0][:, at], 0.0), axis=0, keepdims=True)
            count = jnp.sum(jnp.where(hot, look[1][:, at], 0.0), axis=0, keepdims=True)
            part = fraction[i : i + 1, :] if i < 8 else fraction[9:10, :]
            probs.append((start + part * count) / total)
        probs = jnp.concatenate(probs + [jnp.full((7, 128), 0.5, F32)], axis=0)
        found = ROOT_TWO * quantile(2.0 * jnp.clip(probs, 0.01, 0.99) - 1.0)
        scores[...] = found[0:8, :]
        z = dot3(jnp.broadcast_to(found[8:9, :], (8, 128)), inverse, NT)
        solved[...] = z
        diagonal = jnp.sum(jnp.where(level == across, inverse, 0.0), axis=0, keepdims=True)
        terms_ref[0] = -2.0 * jnp.sum(jnp.log(diagonal))
        terms_ref[1] = jnp.sum(z[0:1, :] * z[0:1, :])

    panel = dot3(rows_ref[...], inverse, NT)
    panel_ref[...] = panel
    high, low = split2(panel)
    update = lax.dot_general(
        jnp.concatenate([high, high, low], axis=1), cols_panel[...], NN, preferred_element_type=F32
    )
    for b in range(8):
        at = pl.ds(b, 128, stride=8)
        trailing_ref[at, :] = matrix_ref[at, :] - update[:, b * 128 : (b + 1) * 128]
    z = solved[...]
    moved = scores[pl.ds(a, 1), :] - dot3(z, panel, NT)[0:1, :]
    k = k_ref[0]
    is_pivot = (lax.axis_index("row") == k % N) & (a == k // N)
    scores_ref[pl.ds(a, 1), :] = jnp.where(is_pivot, z[0:1, :], moved)


def update(k, matrix, rows, cols, inverse, hist, sites, pivot):
    shape = lambda *s: jax.ShapeDtypeStruct(s, F32)
    whole = lambda *s: pl.BlockSpec(s, lambda a: (0,) * len(s))
    smem = pl.BlockSpec(memory_space=pltpu.SMEM)
    return pl.pallas_call(
        update_kernel,
        grid=(8,),
        out_shape=(shape(8192, 128), shape(1024, 128), shape(8, 128), shape(2)),
        in_specs=[
            smem,
            pl.BlockSpec((1024, 128), lambda a: (a, 0)),
            pl.BlockSpec((128, 128), lambda a: (a, 0)),
            whole(8, 128, 128),
            whole(128, 128),
            whole(128, 128),
            whole(3, 8, 128),
            whole(8, 128),
        ],
        out_specs=(
            pl.BlockSpec((1024, 128), lambda a: (a, 0)),
            pl.BlockSpec((128, 128), lambda a: (a, 0)),
            whole(8, 128),
            smem,
        ),
        scratch_shapes=[
            pltpu.VMEM((384, 1024), BF16),
            pltpu.VMEM((8, 128), F32),
            pltpu.VMEM((8, 128), F32),
        ],
        compiler_params=pltpu.CompilerParams(vmem_limit_bytes=24 * MIB),
        name="update",
    )(k, matrix, rows, cols, inverse, hist, sites, pivot)


def on_device(
    panel_index,
    coords,
    region_ids,
    nugget,
    variance,
    length,
    correction,
    bin_index,
    fraction,
    weights,
):
    coords = coords.reshape(2, 8, 128)
    args = (
        panel_index,
        nugget,
        variance,
        length,
        coords,
        coords,
        region_ids.reshape(8, 128),
        bin_index.reshape(8, 8),
        fraction.reshape(8, 8),
        weights.reshape(8, 8),
        correction.reshape(8192, 128),
    )
    branches = [functools.partial(exchange, d) for d in range(N)]
    moved = lax.switch(panel_index[0] % N, branches, *args)
    trailing, panel, scores, terms = update(panel_index, *moved)
    return (
        trailing.reshape(8, 1, 128, 8, 1, 128),
        panel.reshape(8, 1, 128, 128),
        scores.reshape(8, 1, 128),
        terms,
    )


def solution(mesh):
    in_specs = (
        P(),
        P(None, None, "row", None),
        P(None, "row", None),
        P(),
        P(),
        P(),
        P(None, "row", None, None, "col", None),
        P(None, "row", "col", None),
        P(None, "row", "col", None),
        P(None, "row", "col", None),
    )
    out_specs = (
        P(None, "row", None, None, "col", None),
        P(None, "row", None, None),
        P(None, "row", None),
        P(),
    )
    return jax.shard_map(
        on_device, mesh=mesh, in_specs=in_specs, out_specs=out_specs, check_vma=False
    )
```

time: 457 us -> 49.8 us (0.11)
  waiting for transfers between devices: 207 us -> 0 us
  blocking collectives: 174 us -> 0 us
  Pallas kernels: 0 us -> 47.7 us
  other arithmetic: 36.3 us -> 0 us
  between operations: 16.6 us -> 1.48 us
  matrix products: 11.7 us -> 0 us
  local copies, waits for them, and re-layouts: 10.7 us -> 0 us
    psum x2 -> x0, waiting for transfers between devices: 207 us -> none  [from_root(): return lax.psum(block, axis)]
    psum x3 -> x0, blocking collectives: 139 us -> none  [the longest x1 78.9 us: on_device(): hist = lax.psum(local_hist, ('row', 'col'))]
    pallas_call x0 -> x2, Pallas kernels: none -> 47.7 us  [the longest x1 38.1 us: exchange(): pl.pallas_call(functools.partial(exchange_kernel, d), out_shape=(shape(81...]
    all_gather x2 -> x0, blocking collectives: 34.9 us -> none  [the longest x1 19.5 us: on_device(): every_site = lax.all_gather(coords, 'row', axis=2, tiled=True)]
    another operation x8 -> x0, other arithmetic: 24.4 us -> none  [the longest x3 12.4 us: pivot_factor(): factor = jnp.linalg.cholesky(safe_block)]
    dot_general x6 -> x0, matrix products: 10.8 us -> none  [the longest x1 5.48 us: on_device(): trailing = local_matrix - jnp.dot(rows_panel, cols_panel.T, precision=HIGH)]
    unnamed x14 -> x0, local copies, waits for them, and re-layouts: 6.87 us -> none
    sub x1 -> x0, other arithmetic: 5.35 us -> none  [on_device(): local_matrix - correction.reshape(row_tiles * tile, col_tiles * tile)]
  transfers between devices with their start and end apart: 3 -> 0, of which waited for: 2 -> 0; matrix products, arithmetic and copies ran while one was open for 3% -> 0% of each run, Pallas kernels for 0% -> 0%
where the time goes in v1:
time: 49.8 us; the launch traced here: 49.4 us
  Pallas kernels  47.7 us (96%)
  between operations  1.48 us (3%)
    pallas_call x1, Pallas kernels, exchange(): pl.pallas_call(functools.partial(exchange_kernel, d), out_shape=(shape(81...  38.1 us
    pallas_call x1, Pallas kernels, update(): pl.pallas_call(update_kernel, grid=(8,), out_shape=(shape(8192, 128), sha...  9.58 us

profile of v1, /device:TPU:1, one launch (start us, length us, event | category | flops | bytes accessed | tf_op | source)
XLA Modules:
  0.0 49.4 jit_solution(2868630442305113689)
XLA Ops:
  1.3 38.4 %conditional.1 = ((f32[8192,128]{1,0:T(8,128)}, f32[1024,128]{1,0:T(8,128)S(1)}, f32[8,128,128]{2,1,0:T(8,128)S(1)}, f32[128,128]{1,0:T(8,128)S(1)}, f32[128,128...) conditional(s32[]{:T(128)} %clamp.3, (s32[1]{0:T(128)}, ...), branch_computations={%region_0.1_spmd, %region_1.2_spmd, %region_2.3_spmd, %region_3.4_... | conditional | bytes 8 | solution.py:802
  1.3 38.1 %exchange.21 = (f32[8192,128]{1,0:T(8,128)}, f32[1024,128]{1,0:T(8,128)S(1)}, f32[8,128,128]{2,1,0:T(8,128)S(1)}, f32[128,128]{1,0:T(8,128)S(1)}, f32[128,128]{1...) custom-call(s32[1]{0:T(128)} %get-tuple-element.370.k_ref, f32[16]{0:T(128)} %get-tuple-element.371.nugget_ref, ...), custom_call_target="tpu_custom_call" | custom-call | tf_op jit(solution)/shard_map/cond/branch_5_fun/exchange/pallas_call | solution.py:592
  39.7 9.6 %update.1 = (f32[8192,128]{1,0:T(8,128)}, f32[1024,128]{1,0:T(8,128)}, f32[8,128]{1,0:T(8,128)}, f32[2]{0:T(128)}) custom-call(s32[1]{0:T(128)} %copy.129.k_ref, f32[8192,128]{1,0:T(8,128)} %get-tuple-element.495.matrix_ref, f32[1024,128]{1,0:T(8,128)S(1)} %get-tuple-element.496.rows_ref, f32[8,128,128]{2,1,0:T(8,128)S(1)} %get-tuple-element.497.cols_ref, ...), custom_call_target="tpu_custom_call" | custom-call | tf_op jit(solution)/shard_map/update/pallas_call | solution.py:745

commit v2 on v1

--- a/solution.py
+++ b/solution.py
@@ -19,6 +19,8 @@
 NN = (((1,), (0,)), ((), ()))
 TN = (((0,), (0,)), ((), ()))
 PIECE = 64
+EARLY = 2
+KEPT = 4
 MIB = 2**20
 
 
@@ -122,6 +124,49 @@
 
 def exchange_kernel(
     d,
+    k_hbm,
+    nugget_hbm,
+    variance_hbm,
+    length_hbm,
+    coords_hbm,
+    regions_hbm,
+    bins_hbm,
+    fraction_hbm,
+    weights_hbm,
+    corr_hbm,
+    *refs,
+):
+    matrix_out = refs[:8]
+    exchange_body(
+        d,
+        (
+            k_hbm,
+            nugget_hbm,
+            variance_hbm,
+            length_hbm,
+            coords_hbm,
+            regions_hbm,
+            bins_hbm,
+            fraction_hbm,
+            weights_hbm,
+        ),
+        corr_hbm,
+        matrix_out,
+        *refs[8:],
+    )
+
+
+def exchange_body(
+    d,
+    small_hbm,
+    corr_hbm,
+    matrix_out,
+    rows_out,
+    cols_out,
+    inverse_out,
+    hist_out,
+    sites_out,
+    pivot_out,
     k_ref,
     nugget_ref,
     variance_ref,
@@ -132,14 +177,6 @@
     bins_ref,
     fraction_ref,
     weights_ref,
-    corr_hbm,
-    matrix_hbm,
-    rows_out,
-    cols_out,
-    inverse_out,
-    hist_out,
-    sites_out,
-    pivot_out,
     corr,
     row_raw,
     col_raw,
@@ -148,25 +185,36 @@
     factor_rx,
     col_sites,
     pivot_info,
-    obs,
     hist,
     hist_rx,
+    hist_sum,
+    hist_rx2,
     hist_all,
-    sites,
     pivot_obs,
     in_sem,
+    small_sem,
     out_sem,
     send,
     recv,
     row_recv,
 ):
+    (
+        k_hbm,
+        nugget_hbm,
+        variance_hbm,
+        length_hbm,
+        coords_hbm,
+        regions_hbm,
+        bins_hbm,
+        fraction_hbm,
+        weights_hbm,
+    ) = small_hbm
     r = lax.axis_index("row")
     c = lax.axis_index("col")
     sibling = c + 1 - 2 * lax.rem(c, 2)
-    tile_at = jnp.full((128, 128), k_ref[0] // N, I32)
     (
-        S_SITES, S_PIVOT, S_OBS, S_F1, S_F2, S_F3, S_H2, S_H3, S_PO, S_R1, S_R2, S_R3, S_C1, S_C2,
-    ) = range(14)
+        S_SITES, S_PIVOT, S_OBS, S_F1, S_F2, S_F3, S_H2, S_H3, S_PO, S_R1, S_R2, S_R3, S_C1, S_C2, S_H1,
+    ) = range(15)
 
     def row_peer(i):
         return lax.rem(r + i, N)
@@ -208,18 +256,63 @@
 
     each_peer(greet)
     load = pltpu.make_async_copy(corr_hbm, corr, in_sem)
+    small = [
+        pltpu.make_async_copy(src, dst, small_sem.at[i])
+        for i, (src, dst) in enumerate(
+            (
+                (coords_hbm, coords_s),
+                (coords_hbm, coords_ref),
+                (regions_hbm, regions_ref),
+                (bins_hbm, bins_ref),
+                (fraction_hbm, fraction_ref),
+                (weights_hbm, weights_ref),
+                (k_hbm, k_ref),
+                (nugget_hbm, nugget_ref),
+                (variance_hbm, variance_ref),
+                (length_hbm, length_ref),
+            )
+        )
+    ]
+    for copy in small:
+        copy.start()
     load.start()
-
+    for copy in small:
+        copy.wait()
+
+    tile_at = jnp.full((128, 128), k_ref[0] // N, I32)
     factor = ROOT_THREE / length_ref[0]
     variance = variance_ref[0]
     regions = regions_ref[...]
     nugget = jnp.zeros((8, 128), F32)
     for g in range(NREG):
         nugget = jnp.where(regions == g, nugget_ref[g], nugget)
-    obs[0] = jnp.concatenate(
+    obs = jnp.concatenate(
         [bins_ref[...].astype(F32), fraction_ref[...], weights_ref[...], jnp.zeros((8, 104), F32)],
         axis=1,
     )
+    lane = iota((8, 128), 1)
+    level = iota((128, 128), 0)
+
+    def one_row(x):
+        spread = pltpu.roll(x, 0, 1, stride=8, stride_axis=0)
+        return jnp.sum(jnp.where(lane // 8 == iota((8, 128), 0), spread, 0.0), axis=0, keepdims=True)
+
+    own_bins_f = one_row(obs)
+    own_fraction = one_row(pltpu.roll(obs, 128 - 8, 1))
+    own_weights = one_row(pltpu.roll(obs, 128 - 16, 1))
+    own_bins = own_bins_f.astype(I32)
+    weighted = jnp.where(level == (own_bins // 256) * 8 + (own_bins // 128) % 2, own_weights, 0.0)
+    wh, wl = split2(weighted)
+    low = (level == own_bins % 128).astype(F32).astype(BF16)
+    counts = lax.dot_general(
+        jnp.concatenate([wh, wl], axis=1),
+        jnp.concatenate([low, low], axis=1),
+        NT,
+        preferred_element_type=F32,
+    )
+    own_row = jnp.where(lane[0:1] < 64, own_bins_f, pltpu.roll(jnp.broadcast_to(own_fraction, (8, 128)), 64, 1)[0:1])
+    hist[...] = jnp.where(level % 8 == 2, own_row, counts)
+
     pad = jnp.zeros((120, 128), F32)
     x_rows = jnp.transpose(jnp.concatenate([coords_ref[0], pad], axis=0)) * factor
     y_rows = jnp.transpose(jnp.concatenate([coords_ref[1], pad], axis=0)) * factor
@@ -287,15 +380,6 @@
 
     pl.semaphore_wait(barrier, 2 * (N - 1))
 
-    @pl.when(r == d)
-    def _():
-        each_peer(lambda i: send_to(pivot_info, pivot_info, S_PIVOT, (row_peer(i), c)))
-
-    @pl.when(r == c)
-    def _():
-        each_peer(lambda i: send_to(coords_ref, col_sites, S_SITES, (row_peer(i), c)))
-        col_sites[...] = coords_ref[...]
-
     @pl.when((r == d) & (c == d))
     def _():
         each_peer(
@@ -304,8 +388,6 @@
             )
         )
 
-    each_peer(lambda i: send_to(obs.at[0], obs.at[i], S_OBS, (r, col_peer(i))))
-
     @pl.when(r == d)
     def _():
         each_peer(
@@ -314,6 +396,8 @@
             )
         )
 
+    each_peer(lambda i: send_to(rows8(hist, col_peer(i)), hist_rx.at[i], S_H1, (r, col_peer(i))))
+
     @pl.when(c == d)
     def _():
         each_peer(
@@ -322,6 +406,15 @@
             )
         )
 
+    @pl.when(r == c)
+    def _():
+        each_peer(lambda i: send_to(coords_ref, col_sites, S_SITES, (row_peer(i), c)))
+        col_sites[...] = coords_ref[...]
+
+    @pl.when(r == d)
+    def _():
+        each_peer(lambda i: send_to(pivot_info, pivot_info, S_PIVOT, (row_peer(i), c)))
+
     @pl.when((r == d) & (c != d))
     def _():
         wait(rows8(factor_rx, c), recv.at[S_F1])
@@ -332,110 +425,30 @@
             lambda i: send_to(rows8(factor_rx, c), rows8(factor_rx, c), S_F2, (row_peer(i), c))
         )
 
-    def share_row(i):
+    def share_row(i, carry):
         to = col_peer(2 * i)
 
         @pl.when(to != d)
         def _():
             send_to(piece(row_raw, c), piece(row_raw, c), S_R2, (r, to), row_recv.at[c // 2])
 
+        return carry
+
     @pl.when(c != d)
     def _():
         wait(piece(row_raw, c), recv.at[S_R1])
 
-    def share_row_step(i, carry):
-        share_row(i)
-        return carry
-
-    lax.fori_loop(1, 8, share_row_step, 0)
+    lax.fori_loop(1, 8, share_row, 0)
 
     @pl.when(sibling != d)
     def _():
         send_to(piece(row_raw, c), piece(row_raw, c), S_R3, (r, sibling))
 
-    @pl.when(r != d)
-    def _():
-        wait(piece(col_raw, r), recv.at[S_C1])
-
-    def share_col(i):
-        @pl.when(row_peer(i) != d)
-        def _():
-            send_to(piece(col_raw, r), piece(col_raw, r), S_C2, (row_peer(i), c))
-
-    each_peer(share_col)
-
-    wait(obs.at[pl.ds(1, 15)], recv.at[S_OBS])
-    lane = iota((8, 128), 1)
-
-    def unpack(i, found):
-        source = lax.rem(c - i + N, N)
-        packed = obs[i]
-        here = (lane // 8) == source
-        return tuple(
-            jnp.where(here, pltpu.roll(packed, lax.rem(8 * source - 8 * j + 128, 128), 1), found[j])
-            for j in range(3)
-        )
-
-    found = lax.fori_loop(0, N, unpack, tuple(jnp.zeros((8, 128), F32) for _ in range(3)))
-    for j in range(3):
-        sites[j] = found[j]
-
-    @pl.when(r == d)
-    def _():
-        pivot_obs[...] = jnp.concatenate(
-            [
-                pick_row(found[0]),
-                pick_row(found[1]),
-                jnp.zeros((6, 128), F32),
-            ],
-            axis=0,
-        )
-        each_peer(lambda i: send_to(pivot_obs, pivot_obs, S_PO, (row_peer(i), c)))
-
-    level = iota((128, 128), 0)
-
-    def count(a, total):
-        bins_i = sites[0, pl.ds(a, 1), :].astype(I32)
-        high_i = (bins_i // 256) * 8 + (bins_i // 128) % 2
-        weighted = jnp.where(level == high_i, sites[2, pl.ds(a, 1), :], 0.0)
-        wh, wl = split2(weighted)
-        low = (level == bins_i % 128).astype(F32).astype(BF16)
-        return total + lax.dot_general(
-            jnp.concatenate([wh, wl], axis=1),
-            jnp.concatenate([low, low], axis=1),
-            NT,
-            preferred_element_type=F32,
-        )
-
-    hist[...] = lax.fori_loop(0, 8, count, jnp.zeros((128, 128), F32))
-    each_peer(lambda i: send_to(rows8(hist, c), hist_rx.at[i], S_H2, (row_peer(i), c)))
-
-    @pl.when(r != d)
-    def _():
-        wait(rows8(factor_rx, c), recv.at[S_F2])
-
-    each_peer(lambda i: send_to(rows8(factor_rx, c), rows8(factor_rx, c), S_F3, (r, col_peer(i))))
-
-    def pass_on(i):
-        source = lax.rem(c + 16 - 2 * i, N)
-        wait(piece(row_raw, source), row_recv.at[source // 2])
-
-        @pl.when(sibling != d)
-        def _():
-            send_to(piece(row_raw, source), piece(row_raw, source), S_R3, (r, sibling))
-
-    def pass_own(i):
-        source = lax.rem(c + 16 - 2 * i, N)
-        send_to(piece(row_raw, source), piece(row_raw, source), S_R3, (r, sibling))
-
-    def pass_piece(i):
-        @pl.when(c != d)
-        def _():
-            pass_on(i)
-
-        @pl.when(c == d)
-        def _():
-            pass_own(i)
+    wait(hist_rx.at[pl.ds(1, 15)], recv.at[S_H1])
+    own = pl.ds(pl.multiple_of(c * 8, 8), 8)
+    summed = lax.fori_loop(1, N, lambda i, total: total + hist_rx[i], hist[own, :])
+    hist_sum[...] = jnp.where(iota((8, 128), 0) < 2, summed, 0.0)
+    each_peer(lambda i: send_to(hist_sum, hist_rx2.at[i], S_H2, (row_peer(i), c)))
 
     @pl.when(r != c)
     def _():
@@ -446,7 +459,7 @@
     place = iota((8, 128), 0) * 128 + lane
     own_nugget = jnp.where(r == c, nugget, 0.0)
 
-    def form(a, carry_a):
+    def form(a):
         def eight(q, carry):
             for u in range(8):
                 t = q * 8 + u
@@ -459,28 +472,100 @@
             return carry
 
         lax.fori_loop(0, 16, eight, 0)
-        at = pl.ds(pl.multiple_of(a * 1024, 1024), 1024)
-        pltpu.make_async_copy(corr.at[at], matrix_hbm.at[at], out_sem).start()
-
-
-        @pl.when(a == 2)
+        for b in range(8):
+
+            @pl.when(a == b)
+            def _():
+                at = pl.ds(b * 1024, 1024)
+                pltpu.make_async_copy(corr.at[at], matrix_out[b], out_sem).start()
+
+    lax.fori_loop(0, EARLY, lambda a, carry: (form(a), carry)[1], 0)
+
+    @pl.when(r != d)
+    def _():
+        wait(piece(col_raw, r), recv.at[S_C1])
+
+    def share_col(i):
+        @pl.when(row_peer(i) != d)
         def _():
-            wait(hist_rx.at[pl.ds(1, 15)], recv.at[S_H2])
-            own = pl.ds(pl.multiple_of(c * 8, 8), 8)
+            send_to(piece(col_raw, r), piece(col_raw, r), S_C2, (row_peer(i), c))
+
+    each_peer(share_col)
+
+    @pl.when(r != d)
+    def _():
+        wait(rows8(factor_rx, c), recv.at[S_F2])
+
+    each_peer(lambda i: send_to(rows8(factor_rx, c), rows8(factor_rx, c), S_F3, (r, col_peer(i))))
+
+    hist_rx[0] = hist[own, :]
+
+    def unpack(i, found):
+        source = lax.rem(c - i + N, N)
+        packed = jnp.broadcast_to(hist_rx[i][2:3, :], (8, 128))
+        spread = pltpu.roll(packed, 0, 1, stride=8, stride_axis=0)
+        here = (lane // 8) == source
+        return tuple(
+            jnp.where(
+                here,
+                pltpu.roll(spread, lax.rem(8 * source + 64 * j + 72, 128), 1),
+                found[j],
+            )
+            for j in range(2)
+        )
+
+    found = lax.fori_loop(0, N, unpack, (jnp.zeros((8, 128), F32), jnp.zeros((8, 128), F32)))
+    found = [jnp.concatenate([x[7 - a : 8 - a] for a in range(8)], axis=0) for x in found]
+    for j in range(2):
+        sites_out[j] = found[j]
+
+    @pl.when(r == d)
+    def _():
+        pivot_obs[...] = jnp.concatenate(
+            [pick_row(found[0]), pick_row(found[1]), jnp.zeros((6, 128), F32)], axis=0
+        )
+        each_peer(lambda i: send_to(pivot_obs, pivot_obs, S_PO, (row_peer(i), c)))
+
+    def pass_on(i):
+        source = lax.rem(c + 16 - 2 * i, N)
+        wait(piece(row_raw, source), row_recv.at[source // 2])
+
+        @pl.when(sibling != d)
+        def _():
+            send_to(piece(row_raw, source), piece(row_raw, source), S_R3, (r, sibling))
+
+    def pass_own(i):
+        source = lax.rem(c + 16 - 2 * i, N)
+        send_to(piece(row_raw, source), piece(row_raw, source), S_R3, (r, sibling))
+
+    def pass_piece(i):
+        @pl.when(c != d)
+        def _():
+            pass_on(i)
+
+        @pl.when(c == d)
+        def _():
+            pass_own(i)
+
+    def later(a, carry):
+        form(a)
+
+        @pl.when(a == EARLY)
+        def _():
+            wait(hist_rx2.at[pl.ds(1, 15)], recv.at[S_H2])
             hist_all[own, :] = lax.fori_loop(
-                1, N, lambda i, total: total + hist_rx[i], hist[own, :]
+                1, N, lambda i, total: total + hist_rx2[i], hist_sum[...]
             )
             each_peer(
                 lambda i: send_to(rows8(hist_all, c), rows8(hist_all, c), S_H3, (r, col_peer(i)))
             )
 
-        @pl.when(a >= 1)
-        def _():
-            pass_piece(a)
-
-        return carry_a
-
-    lax.fori_loop(0, 8, form, 0)
+        pass_piece(a - 1)
+
+        return carry
+
+    lax.fori_loop(EARLY, 8, later, 0)
+    lax.fori_loop(7, 8, lambda i, carry: (pass_piece(i), carry)[1], 0)
 
     @pl.when(r != d)
     def _():
@@ -519,7 +604,6 @@
         return carry
 
     lax.fori_loop(0, 8, less_cols, 0)
-    sites_out[...] = sites[...]
     pivot_out[...] = pivot_obs[...]
     wait(factor_rx.at[pl.ds(0, 120)], recv.at[S_F3])
     inverse_out[...] = factor_rx[...]
@@ -564,7 +648,7 @@
     def _():
         sent(row_raw.at[pl.ds(0, 15 * PIECE)], S_R1)
 
-    for which in (S_OBS, S_F3, S_H2, S_H3):
+    for which in (S_F3, S_H1, S_H2, S_H3):
         sent(hist.at[pl.ds(0, 120)], which)
 
     same_place = lax.rem(c, 2) == d % 2
@@ -586,23 +670,34 @@
 
 def exchange(d, *args):
     vmem = pl.BlockSpec(memory_space=pltpu.VMEM)
-    smem = pl.BlockSpec(memory_space=pltpu.SMEM)
     hbm = pl.BlockSpec(memory_space=pl.ANY)
+    far = pl.BlockSpec(memory_space=pltpu.HBM)
     shape = lambda *s: jax.ShapeDtypeStruct(s, F32)
     return pl.pallas_call(
         functools.partial(exchange_kernel, d),
         out_shape=(
-            shape(8192, 128),
+            *[shape(1024, 128) for _ in range(KEPT)],
+            *[pltpu.HBM((1024, 128), F32) for _ in range(8 - KEPT)],
             shape(1024, 128),
             shape(8, 128, 128),
             shape(128, 128),
             shape(128, 128),
-            shape(3, 8, 128),
+            shape(2, 8, 128),
             shape(8, 128),
         ),
-        in_specs=[smem] * 5 + [vmem] * 5 + [hbm],
-        out_specs=(hbm,) + (vmem,) * 6,
+        in_specs=[hbm] * 10,
+        out_specs=(vmem,) * KEPT + (far,) * (8 - KEPT) + (vmem,) * 6,
         scratch_shapes=[
+            pltpu.SMEM((1,), I32),
+            pltpu.SMEM((NREG,), F32),
+            pltpu.SMEM((1,), F32),
+            pltpu.SMEM((1,), F32),
+            pltpu.SMEM((2, 8, 128), F32),
+            pltpu.VMEM((2, 8, 128), F32),
+            pltpu.VMEM((8, 128), I32),
+            pltpu.VMEM((8, 8), I32),
+            pltpu.VMEM((8, 8), F32),
+            pltpu.VMEM((8, 8), F32),
             pltpu.VMEM((8192, 128), F32),
             pltpu.VMEM((1024, 128), F32),
             pltpu.VMEM((1024, 128), F32),
@@ -611,20 +706,21 @@
             pltpu.VMEM((128, 128), F32),
             pltpu.VMEM((2, 8, 128), F32),
             pltpu.VMEM((8, 128), F32),
+            pltpu.VMEM((128, 128), F32),
+            pltpu.VMEM((N, 8, 128), F32),
+            pltpu.VMEM((8, 128), F32),
             pltpu.VMEM((N, 8, 128), F32),
             pltpu.VMEM((128, 128), F32),
-            pltpu.VMEM((N, 8, 128), F32),
-            pltpu.VMEM((128, 128), F32),
-            pltpu.VMEM((3, 8, 128), F32),
             pltpu.VMEM((8, 128), F32),
             pltpu.SemaphoreType.DMA,
+            pltpu.SemaphoreType.DMA((10,)),
             pltpu.SemaphoreType.DMA,
-            pltpu.SemaphoreType.DMA((14,)),
-            pltpu.SemaphoreType.DMA((14,)),
+            pltpu.SemaphoreType.DMA((15,)),
+            pltpu.SemaphoreType.DMA((15,)),
             pltpu.SemaphoreType.DMA((8,)),
         ],
         compiler_params=pltpu.CompilerParams(
-            collective_id=d, has_side_effects=True, vmem_limit_bytes=24 * MIB
+            collective_id=d, has_side_effects=True, vmem_limit_bytes=12 * MIB
         ),
         name="exchange",
     )(*args)
@@ -647,129 +743,120 @@
     return p * x
 
 
-def update_kernel(
-    k_ref,
-    matrix_ref,
-    rows_ref,
-    cols_ref,
-    inverse_ref,
-    hist_ref,
-    sites_ref,
-    pivot_ref,
-    trailing_ref,
-    panel_ref,
-    scores_ref,
-    terms_ref,
-    cols_panel,
-    scores,
-    solved,
-):
-    a = pl.program_id(0)
+def update_kernel(k_ref, *refs):
+    matrix_ref = refs[:8]
+    rows_ref, cols_ref, inverse_ref, hist_ref, sites_ref, pivot_ref = refs[8:14]
+    trailing_hbm, panel_hbm, scores_ref, terms_ref = refs[14:18]
+    trailing, panel, late, in_sem, out_sem, panel_sem = refs[18:]
+    loads = [
+        pltpu.make_async_copy(matrix_ref[a], late.at[a - KEPT], in_sem.at[a - KEPT])
+        for a in range(KEPT, 8)
+    ]
+    for load in loads:
+        load.start()
     inverse = inverse_ref[...]
-
-    @pl.when(a == 0)
-    def _():
-        cols = jnp.concatenate([cols_ref[b] for b in range(8)], axis=1)
-        panel = dot3(inverse, cols, NN)
-        high, low = split2(panel)
-        cols_panel[0:128, :] = high
-        cols_panel[128:256, :] = low
-        cols_panel[256:384, :] = high
-
-        counts = hist_ref[...]
-        level = iota((128, 128), 0)
-        across = iota((128, 128), 1)
-        parts = split3(counts)
-        ahead = (across < level).astype(F32).astype(BF16)
-        earlier = (level < across).astype(F32).astype(BF16)
-        above = jnp.zeros((128, 128), F32)
-        along = jnp.zeros((128, 128), F32)
-        for part in parts:
-            above = above + lax.dot_general(ahead, part, NN, preferred_element_type=F32)
-            along = along + lax.dot_general(part, earlier, NN, preferred_element_type=F32)
-        before = jnp.sum(above, axis=1, keepdims=True) + along
-        total = jnp.sum(jnp.sum(counts, axis=1, keepdims=True), axis=0, keepdims=True)
-
-        bins_f = jnp.concatenate([sites_ref[0], pivot_ref[...]], axis=0)
-        fraction = jnp.concatenate([sites_ref[1], pivot_ref[...]], axis=0)
-        bins_i = bins_f.astype(I32)
-        high_i = (bins_i // 256) * 8 + (bins_i // 128) % 2
-        low_i = bins_i % 128
-        high_hot = jnp.concatenate(
-            [(level == high_i[i : i + 1, :]).astype(F32).astype(BF16) for i in range(9)], axis=1
-        )
-        tripled = jnp.concatenate([high_hot] * 3, axis=0)
-        look = [
-            lax.dot_general(
-                jnp.concatenate(split3(table), axis=0), tripled, TN, preferred_element_type=F32
-            )
-            for table in (before, counts)
-        ]
-        probs = []
-        for i in range(9):
-            hot = level == low_i[i : i + 1, :]
-            at = slice(i * 128, (i + 1) * 128)
-            start = jnp.sum(jnp.where(hot, look[0][:, at], 0.0), axis=0, keepdims=True)
-            count = jnp.sum(jnp.where(hot, look[1][:, at], 0.0), axis=0, keepdims=True)
-            part = fraction[i : i + 1, :] if i < 8 else fraction[9:10, :]
-            probs.append((start + part * count) / total)
-        probs = jnp.concatenate(probs + [jnp.full((7, 128), 0.5, F32)], axis=0)
-        found = ROOT_TWO * quantile(2.0 * jnp.clip(probs, 0.01, 0.99) - 1.0)
-        scores[...] = found[0:8, :]
-        z = dot3(jnp.broadcast_to(found[8:9, :], (8, 128)), inverse, NT)
-        solved[...] = z
-        diagonal = jnp.sum(jnp.where(level == across, inverse, 0.0), axis=0, keepdims=True)
-        terms_ref[0] = -2.0 * jnp.sum(jnp.log(diagonal))
-        terms_ref[1] = jnp.sum(z[0:1, :] * z[0:1, :])
-
-    panel = dot3(rows_ref[...], inverse, NT)
-    panel_ref[...] = panel
-    high, low = split2(panel)
-    update = lax.dot_general(
-        jnp.concatenate([high, high, low], axis=1), cols_panel[...], NN, preferred_element_type=F32
+    cols = dot3(inverse, jnp.concatenate([cols_ref[b] for b in range(8)], axis=1), NN)
+    high, low = split2(cols)
+    right = jnp.concatenate([high, low, high], axis=0)
+    whole = dot3(rows_ref[...], inverse, NT)
+    panel[...] = whole
+    whole_high, whole_low = split2(whole)
+    left = jnp.concatenate([whole_high, whole_high, whole_low], axis=1)
+
+    counts = hist_ref[...]
+    level = iota((128, 128), 0)
+    across = iota((128, 128), 1)
+    parts = split3(counts)
+    ahead = (across < level).astype(F32).astype(BF16)
+    earlier = (level < across).astype(F32).astype(BF16)
+    above = jnp.zeros((128, 128), F32)
+    along = jnp.zeros((128, 128), F32)
+    for part in parts:
+        above = above + lax.dot_general(ahead, part, NN, preferred_element_type=F32)
+        along = along + lax.dot_general(part, earlier, NN, preferred_element_type=F32)
+    before = jnp.sum(above, axis=1, keepdims=True) + along
+    total = jnp.sum(jnp.sum(counts, axis=1, keepdims=True), axis=0, keepdims=True)
+
+    bins_f = jnp.concatenate([sites_ref[0], pivot_ref[...]], axis=0)
+    fraction = jnp.concatenate([sites_ref[1], pivot_ref[...]], axis=0)
+    bins_i = bins_f.astype(I32)
+    high_i = (bins_i // 256) * 8 + (bins_i // 128) % 2
+    low_i = bins_i % 128
+    high_hot = jnp.concatenate(
+        [(level == high_i[i : i + 1, :]).astype(F32).astype(BF16) for i in range(9)], axis=1
     )
-    for b in range(8):
-        at = pl.ds(b, 128, stride=8)
-        trailing_ref[at, :] = matrix_ref[at, :] - update[:, b * 128 : (b + 1) * 128]
-    z = solved[...]
-    moved = scores[pl.ds(a, 1), :] - dot3(z, panel, NT)[0:1, :]
+    tripled = jnp.concatenate([high_hot] * 3, axis=0)
+    look = [
+        lax.dot_general(
+            jnp.concatenate(split3(table), axis=0), tripled, TN, preferred_element_type=F32
+        )
+        for table in (before, counts)
+    ]
+    probs = []
+    for i in range(9):
+        hot = level == low_i[i : i + 1, :]
+        at = slice(i * 128, (i + 1) * 128)
+        start = jnp.sum(jnp.where(hot, look[0][:, at], 0.0), axis=0, keepdims=True)
+        count = jnp.sum(jnp.where(hot, look[1][:, at], 0.0), axis=0, keepdims=True)
+        part = fraction[i : i + 1, :] if i < 8 else fraction[9:10, :]
+        probs.append((start + part * count) / total)
+    probs = jnp.concatenate(probs + [jnp.full((7, 128), 0.5, F32)], axis=0)
+    found = ROOT_TWO * quantile(2.0 * jnp.clip(probs, 0.01, 0.99) - 1.0)
+    z = dot3(jnp.broadcast_to(found[8:9, :], (8, 128)), inverse, NT)
+    diagonal = jnp.sum(jnp.where(level == across, inverse, 0.0), axis=0, keepdims=True)
+    terms_ref[0] = -2.0 * jnp.sum(jnp.log(diagonal))
+    terms_ref[1] = jnp.sum(z[0:1, :] * z[0:1, :])
+    moved = dot3(z, whole, NT)
     k = k_ref[0]
-    is_pivot = (lax.axis_index("row") == k % N) & (a == k // N)
-    scores_ref[pl.ds(a, 1), :] = jnp.where(is_pivot, z[0:1, :], moved)
-
-
-def update(k, matrix, rows, cols, inverse, hist, sites, pivot):
+    here = lax.axis_index("row") == k % N
+    for a in range(8):
+        score = found[a : a + 1, :] - moved[0:1, a * 128 : (a + 1) * 128]
+        scores_ref[a : a + 1, :] = jnp.where(here & (k // N == a), z[0:1, :], score)
+
+    panel_copy = pltpu.make_async_copy(panel, panel_hbm, panel_sem)
+    panel_copy.start()
+    for a in range(8):
+        change = lax.dot_general(
+            left[a * 128 : (a + 1) * 128], right, NN, preferred_element_type=F32
+        )
+        block = matrix_ref[a] if a < KEPT else late.at[a - KEPT]
+        if a >= KEPT:
+            loads[a - KEPT].wait()
+        for b in range(8):
+            at = pl.ds(a * 1024 + b, 128, stride=8)
+            before = block[pl.ds(b, 128, stride=8), :]
+            trailing[at, :] = before - change[:, b * 128 : (b + 1) * 128]
+        at = pl.ds(a * 1024, 1024)
+        pltpu.make_async_copy(trailing.at[at], trailing_hbm.at[at], out_sem.at[a]).start()
+
+    panel_copy.wait()
+    for a in range(8):
+        at = pl.ds(a * 1024, 1024)
+        pltpu.make_async_copy(trailing.at[at], trailing_hbm.at[at], out_sem.at[a]).wait()
+
+
+def update(*args):
     shape = lambda *s: jax.ShapeDtypeStruct(s, F32)
-    whole = lambda *s: pl.BlockSpec(s, lambda a: (0,) * len(s))
+    vmem = pl.BlockSpec(memory_space=pltpu.VMEM)
     smem = pl.BlockSpec(memory_space=pltpu.SMEM)
+    hbm = pl.BlockSpec(memory_space=pl.ANY)
+    far = pl.BlockSpec(memory_space=pltpu.HBM)
     return pl.pallas_call(
         update_kernel,
-        grid=(8,),
         out_shape=(shape(8192, 128), shape(1024, 128), shape(8, 128), shape(2)),
-        in_specs=[
-            smem,
-            pl.BlockSpec((1024, 128), lambda a: (a, 0)),
-            pl.BlockSpec((128, 128), lambda a: (a, 0)),
-            whole(8, 128, 128),
-            whole(128, 128),
-            whole(128, 128),
-            whole(3, 8, 128),
-            whole(8, 128),
+        in_specs=[smem] + [vmem] * KEPT + [far] * (8 - KEPT) + [vmem] * 6,
+        out_specs=(hbm, hbm, vmem, smem),
+        scratch_shapes=[
+            pltpu.VMEM((8192, 128), F32),
+            pltpu.VMEM((1024, 128), F32),
+            pltpu.VMEM((8 - KEPT, 1024, 128), F32),
+            pltpu.SemaphoreType.DMA((8 - KEPT,)),
+            pltpu.SemaphoreType.DMA((8,)),
+            pltpu.SemaphoreType.DMA,
         ],
-        out_specs=(
-            pl.BlockSpec((1024, 128), lambda a: (a, 0)),
-            pl.BlockSpec((128, 128), lambda a: (a, 0)),
-            whole(8, 128),
-            smem,
-        ),
-        scratch_shapes=[
-            pltpu.VMEM((384, 1024), BF16),
-            pltpu.VMEM((8, 128), F32),
-            pltpu.VMEM((8, 128), F32),
-        ],
-        compiler_params=pltpu.CompilerParams(vmem_limit_bytes=24 * MIB),
+        compiler_params=pltpu.CompilerParams(vmem_limit_bytes=12 * MIB),
         name="update",
-    )(k, matrix, rows, cols, inverse, hist, sites, pivot)
+    )(*args)
 
 
 def on_device(
@@ -791,7 +878,6 @@
         variance,
         length,
         coords,
-        coords,
         region_ids.reshape(8, 128),
         bin_index.reshape(8, 8),
         fraction.reshape(8, 8),
@@ -799,7 +885,7 @@
         correction.reshape(8192, 128),
     )
     branches = [functools.partial(exchange, d) for d in range(N)]
-    moved = lax.switch(panel_index[0] % N, branches, *args)
+    moved = lax.switch(panel_index[0] & (N - 1), branches, *args)
     trailing, panel, scores, terms = update(panel_index, *moved)
     return (
         trailing.reshape(8, 1, 128, 8, 1, 128),

time: 49.8 us -> 43.2 us (0.87)
  Pallas kernels: 47.7 us -> 40.8 us
    pallas_call x2, Pallas kernels: 47.7 us -> 40.8 us  [the longest x1 33.8 us: exchange(): pl.pallas_call(functools.partial(exchange_kernel, d), out_shape=(*[shape(...]
where the time goes in v2:
time: 43.2 us; the launch traced here: 42.7 us
  Pallas kernels  40.8 us (94%)
  between operations  1.47 us (3%)
  loops' own time  0.46 us (1%)
    pallas_call x1, Pallas kernels, exchange(): pl.pallas_call(functools.partial(exchange_kernel, d), out_shape=(*[shape(...  33.8 us
    pallas_call x1, Pallas kernels, update(): pl.pallas_call(update_kernel, out_shape=(shape(8192, 128), shape(1024, 12...  6.92 us

profile of v2, /device:TPU:1, one launch (start us, length us, event | category | flops | bytes accessed | tf_op | source)
XLA Modules:
  0.0 42.7 jit_solution(16880335733616526599)
XLA Ops:
  1.3 34.3 %conditional.1 = ((f32[1024,128]{1,0:T(8,128)S(1)}, f32[1024,128]{1,0:T(8,128)S(1)}, f32[1024,128]{1,0:T(8,128)S(1)}, f32[1024,128]{1,0:T(8,128)S(1)}, f32[1024,...) conditional(s32[]{:T(128)} %bitcast, (s32[1]{0:T(128)}, ...), branch_computations={%region_0.0_spmd, %region_1.0_spmd, %region_2.0_spmd, %region_3.0_... | conditional | bytes 8 | solution.py:888
  1.3 33.8 %exchange.21 = (f32[1024,128]{1,0:T(8,128)S(1)}, f32[1024,128]{1,0:T(8,128)S(1)}, f32[1024,128]{1,0:T(8,128)S(1)}, f32[1024,128]{1,0:T(8,128)S(1)}, f32[1024,128...) custom-call(s32[1]{0:T(128)} %get-tuple-element.370.k_hbm, ...), custom_call_target="tpu_custom_call" | custom-call | tf_op jit(solution)/shard_map/cond/branch_5_fun/exchange/pallas_call | solution.py:676
  35.6 6.9 %update.1 = (f32[8192,128]{1,0:T(8,128)}, f32[1024,128]{1,0:T(8,128)}, f32[8,128]{1,0:T(8,128)}, f32[2]{0:T(128)}) custom-call(s32[1]{0:T(128)S(6)} %copy.241.k_ref, f32[1024,128]{1,0:T(8,128)S(1)} %get-tuple-element.502.refs_0_, f32[1024,128]{1,0:T(8,128)S(1)} %get-tuple-element.503.refs_1_, f32[1024,128]{1,0:T(8,128)S(1)} %get-tuple-element.504.refs_2_, ...), custom_call_target="tpu_custom_call" | custom-call | tf_op jit(solution)/shard_map/update/pallas_call | solution.py:844

commit v3 on v2

--- a/solution.py
+++ b/solution.py
@@ -19,6 +19,7 @@
 NN = (((1,), (0,)), ((), ()))
 TN = (((0,), (0,)), ((), ()))
 PIECE = 64
+MIDDLE = 3
 EARLY = 2
 KEPT = 4
 MIB = 2**20
@@ -57,12 +58,11 @@
     return (variance + variance * scaled) * jnp.exp(-scaled)
 
 
-def factor_inverse(work, inv):
+def factor_inverse(work, inv, start, stop):
     nb = 16
     groups = nb // 8
     sub = iota((8, 128), 0)
     lane = iota((nb, 128), 1)
-    inv[...] = (iota((128, 128), 0) == iota((128, 128), 1)).astype(F32)
 
     def block(p, carry):
         rows_k = [work[8 * g : 8 * g + 8, :] for g in range(groups)]
@@ -119,7 +119,7 @@
         inv[128 - nb :, :] = done
         return carry
 
-    lax.fori_loop(0, 128 // nb, block, 0)
+    lax.fori_loop(start, stop, block, 0)
 
 
 def exchange_kernel(
@@ -375,45 +375,59 @@
             return carry
 
         lax.fori_loop(0, 4, own_tile, 0)
-        factor_inverse(work, inverse)
+        inverse[...] = jnp.where(diagonal, 1.0, 0.0)
+
+    def half(stage, carry):
+        @pl.when((r == d) & (c == d))
+        def _():
+            factor_inverse(work, inverse, 4 * stage, 4 * stage + 4)
+
+        @pl.when(stage == 0)
+        def _():
+            first_sends()
+
+        return carry
+
+    def first_sends():
+        pl.semaphore_wait(barrier, 2 * (N - 1))
+
+        @pl.when(r == d)
+        def _():
+            each_peer(
+                lambda i: send_to(
+                    piece(col_raw, row_peer(i)), piece(col_raw, row_peer(i)), S_C1, (row_peer(i), c)
+                )
+            )
+
+        each_peer(lambda i: send_to(rows8(hist, col_peer(i)), hist_rx.at[i], S_H1, (r, col_peer(i))))
+
+        @pl.when(c == d)
+        def _():
+            each_peer(
+                lambda i: send_to(
+                    piece(row_raw, col_peer(i)), piece(row_raw, col_peer(i)), S_R1, (r, col_peer(i))
+                )
+            )
+
+        @pl.when(r == c)
+        def _():
+            each_peer(lambda i: send_to(coords_ref, col_sites, S_SITES, (row_peer(i), c)))
+            col_sites[...] = coords_ref[...]
+
+        @pl.when(r == d)
+        def _():
+            each_peer(lambda i: send_to(pivot_info, pivot_info, S_PIVOT, (row_peer(i), c)))
+
+    lax.fori_loop(0, 2, half, 0)
+
+    @pl.when((r == d) & (c == d))
+    def _():
         factor_rx[8 * d : 8 * d + 8, :] = inverse[8 * d : 8 * d + 8, :]
-
-    pl.semaphore_wait(barrier, 2 * (N - 1))
-
-    @pl.when((r == d) & (c == d))
-    def _():
         each_peer(
             lambda i: send_to(
                 rows8(inverse, col_peer(i)), rows8(factor_rx, col_peer(i)), S_F1, (r, col_peer(i))
             )
         )
-
-    @pl.when(r == d)
-    def _():
-        each_peer(
-            lambda i: send_to(
-                piece(col_raw, row_peer(i)), piece(col_raw, row_peer(i)), S_C1, (row_peer(i), c)
-            )
-        )
-
-    each_peer(lambda i: send_to(rows8(hist, col_peer(i)), hist_rx.at[i], S_H1, (r, col_peer(i))))
-
-    @pl.when(c == d)
-    def _():
-        each_peer(
-            lambda i: send_to(
-                piece(row_raw, col_peer(i)), piece(row_raw, col_peer(i)), S_R1, (r, col_peer(i))
-            )
-        )
-
-    @pl.when(r == c)
-    def _():
-        each_peer(lambda i: send_to(coords_ref, col_sites, S_SITES, (row_peer(i), c)))
-        col_sites[...] = coords_ref[...]
-
-    @pl.when(r == d)
-    def _():
-        each_peer(lambda i: send_to(pivot_info, pivot_info, S_PIVOT, (row_peer(i), c)))
 
     @pl.when((r == d) & (c != d))
     def _():
@@ -491,12 +505,6 @@
             send_to(piece(col_raw, r), piece(col_raw, r), S_C2, (row_peer(i), c))
 
     each_peer(share_col)
-
-    @pl.when(r != d)
-    def _():
-        wait(rows8(factor_rx, c), recv.at[S_F2])
-
-    each_peer(lambda i: send_to(rows8(factor_rx, c), rows8(factor_rx, c), S_F3, (r, col_peer(i))))
 
     hist_rx[0] = hist[own, :]
 
@@ -547,25 +555,36 @@
         def _():
             pass_own(i)
 
+    def form_and_pass(a, carry):
+        form(a)
+        pass_piece(a - 1)
+        return carry
+
     def later(a, carry):
-        form(a)
-
-        @pl.when(a == EARLY)
-        def _():
-            wait(hist_rx2.at[pl.ds(1, 15)], recv.at[S_H2])
-            hist_all[own, :] = lax.fori_loop(
-                1, N, lambda i, total: total + hist_rx2[i], hist_sum[...]
-            )
-            each_peer(
-                lambda i: send_to(rows8(hist_all, c), rows8(hist_all, c), S_H3, (r, col_peer(i)))
-            )
-
-        pass_piece(a - 1)
-
+        @pl.when(a == MIDDLE)
+        def _():
+            last_hops()
+
+        form_and_pass(a, carry)
         return carry
 
+    def last_hops():
+        @pl.when(r != d)
+        def _():
+            wait(rows8(factor_rx, c), recv.at[S_F2])
+
+        each_peer(lambda i: send_to(rows8(factor_rx, c), rows8(factor_rx, c), S_F3, (r, col_peer(i))))
+
+        wait(hist_rx2.at[pl.ds(1, 15)], recv.at[S_H2])
+        hist_all[own, :] = lax.fori_loop(
+            1, N, lambda i, total: total + hist_rx2[i], hist_sum[...]
+        )
+        each_peer(
+            lambda i: send_to(rows8(hist_all, c), rows8(hist_all, c), S_H3, (r, col_peer(i)))
+        )
+
     lax.fori_loop(EARLY, 8, later, 0)
-    lax.fori_loop(7, 8, lambda i, carry: (pass_piece(i), carry)[1], 0)
+    pass_piece(7)
 
     @pl.when(r != d)
     def _():

time: 43.2 us -> 43.1 us (level)
  the two profiles are of different devices: /device:TPU:1 before, /device:TPU:3 now
where the time goes in v3:
time: 43.1 us; the launch traced here: 42.5 us
  Pallas kernels  40.5 us (94%)
  between operations  1.47 us (3%)
  loops' own time  0.46 us (1%)
    pallas_call x1, Pallas kernels, exchange(): pl.pallas_call(functools.partial(exchange_kernel, d), out_shape=(*[shape(...  33.6 us
    pallas_call x1, Pallas kernels, update(): pl.pallas_call(update_kernel, out_shape=(shape(8192, 128), shape(1024, 12...  6.93 us

profile of v3, /device:TPU:3, one launch (start us, length us, event | category | flops | bytes accessed | tf_op | source)
XLA Modules:
  0.0 42.5 jit_solution(15391573024922693105)
XLA Ops:
  1.3 34.1 %conditional.1 = ((f32[1024,128]{1,0:T(8,128)S(1)}, f32[1024,128]{1,0:T(8,128)S(1)}, f32[1024,128]{1,0:T(8,128)S(1)}, f32[1024,128]{1,0:T(8,128)S(1)}, f32[1024,...) conditional(s32[]{:T(128)} %bitcast, (s32[1]{0:T(128)}, ...), branch_computations={%region_0.0_spmd, %region_1.0_spmd, %region_2.0_spmd, %region_3.0_... | conditional | bytes 8 | solution.py:907
  1.3 33.6 %exchange.16 = (f32[1024,128]{1,0:T(8,128)S(1)}, f32[1024,128]{1,0:T(8,128)S(1)}, f32[1024,128]{1,0:T(8,128)S(1)}, f32[1024,128]{1,0:T(8,128)S(1)}, f32[1024,128...) custom-call(s32[1]{0:T(128)} %get-tuple-element.320.k_hbm, ...), custom_call_target="tpu_custom_call" | custom-call | tf_op jit(solution)/shard_map/cond/branch_0_fun/exchange/pallas_call | solution.py:695
  35.3 6.9 %update.1 = (f32[8192,128]{1,0:T(8,128)}, f32[1024,128]{1,0:T(8,128)}, f32[8,128]{1,0:T(8,128)}, f32[2]{0:T(128)}) custom-call(s32[1]{0:T(128)S(6)} %copy.241.k_ref, f32[1024,128]{1,0:T(8,128)S(1)} %get-tuple-element.502.refs_0_, f32[1024,128]{1,0:T(8,128)S(1)} %get-tuple-element.503.refs_1_, f32[1024,128]{1,0:T(8,128)S(1)} %get-tuple-element.504.refs_2_, ...), custom_call_target="tpu_custom_call" | custom-call | tf_op jit(solution)/shard_map/update/pallas_call | solution.py:863
